TPU v7x, 512 devices: a whole 4x8x8 slice. The times are simulated.
512 devices in a mesh: section: 8 (over y), expert: 64 (over x, z, core).
Axes of the slice: x: 4, y: 8, z: 8, core: 2. Of those that a mesh axis runs over, the one named last changes fastest.
Arguments:
- layer_input: bfloat16 [8, 4096, 2048], P('section', 'expert'), may hold values from -6 to 6
- out_grad: bfloat16 [8, 4096, 2048], P('section', 'expert'), may hold values from -6 to 6
- norm_gain: float32 [8, 2048], P('section'), may hold values from 0.5 to 1.5
- expert_ids: int32 [8, 4096, 8], P('section', 'expert'), may hold values from 0 to 127, all different within a row; in each aligned block of 64 rows (0 to 63, 64 to 127, ..., all dimensions but the last counted through in order) at most 8 rows name the same one
- combine: bfloat16 [8, 4096, 8], P('section', 'expert'), may hold values from 0.049804688 to 0.29882812
- w_gate: bfloat16 [8, 12288, 2048], P('section', 'expert'), may hold values from -0.125 to 0.125
- w_up: bfloat16 [8, 12288, 2048], P('section', 'expert'), may hold values from -0.125 to 0.125
- w_down: bfloat16 [8, 12288, 2048], P('section', 'expert'), may hold values from -0.21875 to 0.21875
Outputs:
- passed_grad: bfloat16 [8, 4096, 2048], P('section', 'expert')
- comb_grad: bfloat16 [8, 4096, 8], P('section', 'expert')
- gain_grad: float32 [8, 2048], P('section')
Inputs may be any that keep to these rules, and one draw needn't show every extreme that they name: `expert_ids`: A token names 8 different experts. Within the tokens of one device (aligned blocks of 64 tokens of a section) no expert is named by more than 8 tokens, a bound that some block reaches.
All inputs are finite; a program needn't handle non-finite values.
Results may differ from a plain program's by a relative error of at most 0.0075.
Values may be sent and summed in bfloat16 or wider, within the bound.
A program may use at most 64 MiB of HBM per device.

v0:
```python
import jax
import jax.numpy as jnp
from jax import lax
from jax.sharding import PartitionSpec as P

EXPERTS = 16
CAP = 8
epsilon = 1e-06


def from_behind(block, axis, distance):
    devices = range(lax.axis_size(axis))
    route = [(i - distance, i) for i in devices if i - distance in devices]
    return lax.ppermute(block, axis, route)


def contract_cols(left, right):
    return lax.dot_general(
        left, right, (((1,), (1,)), ((), ())), preferred_element_type=jnp.float32
    )


def exact_rows(left, right):
    return lax.dot_general(
        left,
        right,
        (((0,), (0,)), ((), ())),
        preferred_element_type=jnp.float32,
        precision=lax.Precision.HIGHEST,
    )


def forward_part(rows_x, weight_gate, weight_up, weight_down):
    gate = contract_cols(rows_x, weight_gate)
    upper = contract_cols(rows_x, weight_up)
    sigma = jax.nn.sigmoid(gate)
    active = gate * sigma
    hidden = (active * upper).astype(jnp.bfloat16)
    output = jnp.dot(hidden, weight_down, preferred_element_type=jnp.float32)
    return (gate, upper, sigma, active, hidden, output)


def backward_part(rows_dy, rows_w, early, weight_gate, weight_up, weight_down):
    gate, upper, sigma, active, hidden, output = early
    comb_part = jnp.sum(rows_dy.astype(jnp.float32) * output, axis=-1).astype(jnp.bfloat16)
    scaled = (rows_w.astype(jnp.float32)[:, None] * rows_dy.astype(jnp.float32)).astype(
        jnp.bfloat16
    )
    hidden_grad = contract_cols(scaled, weight_down)
    gate_part = (hidden_grad * upper * sigma * (1.0 + gate * (1.0 - sigma))).astype(jnp.bfloat16)
    up_part = (hidden_grad * active).astype(jnp.bfloat16)
    rows_grad = (
        jnp.dot(gate_part, weight_gate, preferred_element_type=jnp.float32)
        + jnp.dot(up_part, weight_up, preferred_element_type=jnp.float32)
    ).astype(jnp.bfloat16)
    return (rows_grad, comb_part)


def per_device(layer_input, out_grad, norm_gain, expert_ids, combine, w_gate, w_up, w_down):
    inputs = layer_input[0]
    incoming_gradient = out_grad[0]
    scale_factors = norm_gain[0]
    choices = expert_ids[0]
    weights = combine[0]
    weight_gate = w_gate[0]
    weight_up = w_up[0]
    weight_down = w_down[0]
    tokens_here, width = inputs.shape
    top_count = choices.shape[1]
    peers = lax.axis_size("expert")
    sharing = peers // EXPERTS
    route_count = tokens_here * top_count
    slot_total = EXPERTS * CAP
    peer_slots = peers * CAP
    float_values = inputs.astype(jnp.float32)
    reciprocal_norm = lax.rsqrt(
        jnp.mean(float_values * float_values, axis=-1, keepdims=True) + epsilon
    )
    normalized_rows = float_values * reciprocal_norm
    normalized_input = (normalized_rows * scale_factors[None, :]).astype(jnp.bfloat16)
    flat_ids = choices.reshape(route_count)
    onehot = (flat_ids[:, None] == jnp.arange(EXPERTS, dtype=jnp.int32)[None, :]).astype(jnp.int32)
    before = jnp.cumsum(onehot, axis=0) - onehot
    slot = jnp.sum(before * onehot, axis=1)
    target = flat_ids * CAP + slot
    route_pick = (target[None, :] == jnp.arange(slot_total, dtype=jnp.int32)[:, None]).astype(
        jnp.bfloat16
    )
    token_pick = jnp.sum(route_pick.reshape(slot_total, tokens_here, top_count), axis=-1)
    send_x = jnp.dot(token_pick, normalized_input, preferred_element_type=jnp.float32).astype(
        jnp.bfloat16
    )
    send_x = jnp.repeat(send_x.reshape(EXPERTS, CAP, width), sharing, axis=0)
    send_dy = jnp.dot(token_pick, incoming_gradient, preferred_element_type=jnp.float32).astype(
        jnp.bfloat16
    )
    send_dy = jnp.repeat(send_dy.reshape(EXPERTS, CAP, width), sharing, axis=0)
    send_w = jnp.dot(
        route_pick, weights.reshape(route_count, 1), preferred_element_type=jnp.float32
    )
    send_w = jnp.repeat(send_w.astype(jnp.bfloat16).reshape(EXPERTS, CAP), sharing, axis=0)
    early = None
    rows_x, rows_dy, rows_w = (
        lax.all_to_all(send_x, "expert", split_axis=0, concat_axis=0, tiled=True),
        lax.all_to_all(send_dy, "expert", split_axis=0, concat_axis=0, tiled=True),
        lax.all_to_all(send_w, "expert", split_axis=0, concat_axis=0, tiled=True),
    )
    flat_rows = rows_x.reshape(peer_slots, width)
    early = forward_part(flat_rows, weight_gate, weight_up, weight_down)
    rows_grad, comb_part = backward_part(
        rows_dy.reshape(peer_slots, width),
        rows_w.reshape(peer_slots),
        early,
        weight_gate,
        weight_up,
        weight_down,
    )
    back_rows, back_comb = (
        lax.all_to_all(
            rows_grad.reshape(peers, CAP, width), "expert", split_axis=0, concat_axis=0, tiled=True
        ),
        lax.all_to_all(
            comb_part.reshape(peers, CAP), "expert", split_axis=0, concat_axis=0, tiled=True
        ),
    )
    summed_rows = jnp.sum(
        back_rows.reshape(EXPERTS, sharing, CAP, width).astype(jnp.float32), axis=1
    )
    summed_comb = jnp.sum(back_comb.reshape(EXPERTS, sharing, CAP).astype(jnp.float32), axis=1)
    normalized_gradient = exact_rows(
        token_pick.astype(jnp.float32), summed_rows.reshape(slot_total, width)
    )
    comb_out = exact_rows(route_pick.astype(jnp.float32), summed_comb.reshape(slot_total, 1))
    comb_out = comb_out.astype(jnp.bfloat16).reshape(tokens_here, top_count)
    gain_correction = jnp.sum(normalized_gradient * normalized_rows, axis=0)
    scaled_gradient = normalized_gradient * scale_factors[None, :]
    inner_product = jnp.mean(scaled_gradient * normalized_rows, axis=-1, keepdims=True)
    input_gradient = (
        incoming_gradient.astype(jnp.float32)
        + reciprocal_norm * (scaled_gradient - normalized_rows * inner_product)
    ).astype(jnp.bfloat16)
    passed = from_behind(input_gradient, "section", -1)
    gain_total = lax.psum(gain_correction, "expert")
    return (passed[None], comb_out[None], gain_total[None])


def solution(mesh):
    placed = (
        P("section", "expert", None),
        P("section", "expert", None),
        P("section", None),
        P("section", "expert", None),
        P("section", "expert", None),
        P("section", "expert", None),
        P("section", "expert", None),
        P("section", "expert", None),
    )
    return jax.shard_map(
        per_device,
        mesh=mesh,
        in_specs=placed,
        out_specs=(P("section", "expert", None), P("section", "expert", None), P("section", None)),
        check_vma=False,
    )
```

profile of v0, /device:TPU:56, one launch (start us, length us, event | category | flops | bytes accessed | tf_op | source)
XLA Modules:
  0.0 356.8 jit_solution(8759035831997450475)
XLA Ops:
  0.6 0.0 copy-start
  0.6 0.8 copy.33
  1.5 0.1 eq.45
  1.6 0.1 eq.49
  1.7 0.8 copy.37
  2.4 0.1 reshape.157
  2.6 1.2 reduce-window.6
  3.7 0.2 slice_reduce_fusion
  4.0 0.1 fusion.52
  4.1 0.2 fusion.14
  4.2 0.1 reshape.143
  4.4 0.6 copy.38
  5.0 13.8 %all-to-all-start = ((bf16[64,1,8]{2,1,0:T(2,128)(2,1)}), bf16[64,1,8]{2,1,0:T(2,128)(2,1)S(1)}, u32[]{:S(2)}, u32[]{:S(2)}) async-start(bf16[64,1,8]{2,1,0:T(2,128)(2,1)} %copy.38), calls=%async_computation | async-start | bytes 65536 | tf_op jit(solution)/shard_map/all_to_all | solution.py:106
  18.8 0.1 reduce_sum.79
  18.9 1.1 fusion.35
  20.0 0.2 fusion.45
  20.2 1.3 fusion.5
  21.5 6.7 %all-to-all-done = bf16[64,1,8]{2,1,0:T(2,128)(2,1)S(1)} async-done(((bf16[64,1,8]{2,1,0:T(2,128)(2,1)}), bf16[64,1,8]{2,1,0:T(2,128)(2,1)S(1)}, u32[]{:S(2)}, u32[]{:S(2)}) %all-to-all-start) | async-done | bytes 1056 | tf_op jit(solution)/shard_map/all_to_all | solution.py:106
  28.2 1.6 broadcast_in_dim.23
  29.9 4.7 %all-to-all-start.2 = ((bf16[64,8,2048]{2,1,0:T(8,128)(2,1)}), bf16[64,8,2048]{2,1,0:T(8,128)(2,1)S(1)}, u32[]{:S(2)}, u32[]{:S(2)}) async-start(bf16[64,8,2048]{2,1,0:T(8,128)(2,1)} %bitcast.14), calls=%async_computation.2 | async-start | bytes 4194304 | tf_op jit(solution)/shard_map/all_to_all | solution.py:104
  34.6 1.3 fusion.4
  35.8 49.9 %all-to-all-done.2 = bf16[64,8,2048]{2,1,0:T(8,128)(2,1)S(1)} async-done(((bf16[64,8,2048]{2,1,0:T(8,128)(2,1)}), bf16[64,8,2048]{2,1,0:T(8,128)(2,1)S(1)}, u32[]{:S(2)}, u32[]{:S(2)}) %all-to-all-start.2) | async-done | bytes 2097184 | tf_op jit(solution)/shard_map/all_to_all | solution.py:104
  85.7 0.0 copy-start.2
  85.7 1.8 broadcast_in_dim.22
  87.6 0.2 copy-done.2
  87.7 5.9 %all-to-all-start.1 = ((bf16[64,8,2048]{2,1,0:T(8,128)(2,1)}), bf16[64,8,2048]{2,1,0:T(8,128)(2,1)S(1)}, u32[]{:S(2)}, u32[]{:S(2)}) async-start(bf16[64,8,2048]{2,1,0:T(8,128)(2,1)} %bitcast.8), calls=%async_computation.1 | async-start | bytes 4194304 | tf_op jit(solution)/shard_map/all_to_all | solution.py:105
  93.7 0.0 copy-done
  93.7 0.0 copy-start.3
  93.7 0.0 copy-start.5
  93.7 2.6 fusion.9
  96.3 0.0 copy-done.3
  96.3 0.0 copy-done.5
  96.3 1.6 fusion.11
  97.9 46.9 %all-to-all-done.1 = bf16[64,8,2048]{2,1,0:T(8,128)(2,1)S(1)} async-done(((bf16[64,8,2048]{2,1,0:T(8,128)(2,1)}), bf16[64,8,2048]{2,1,0:T(8,128)(2,1)S(1)}, u32[]{:S(2)}, u32[]{:S(2)}) %all-to-all-start.1) | async-done | bytes 2097184 | tf_op jit(solution)/shard_map/all_to_all | solution.py:105
  144.8 0.0 copy-start.7
  144.8 2.1 fusion.7
  146.9 0.0 copy-done.7
  146.9 0.0 copy-start.6
  146.9 0.8 fusion.17
  147.8 0.3 copy-done.6
  148.1 0.8 fusion.3
  148.8 56.9 %all_to_all.30 = bf16[64,8,2048]{2,1,0:T(8,128)(2,1)S(1)} all-to-all(bf16[64,8,2048]{2,1,0:T(8,128)(2,1)S(1)} %fusion.3), channel_id=1, replica_groups=mesh['section'=8,'expert'=64] {'expert'}, dimensions={0} | all-to-all | bytes 4194304 | tf_op jit(solution)/shard_map/all_to_all | solution.py:119
  205.7 0.0 copy-start.1
  205.7 0.0 copy-start.8
  205.7 0.0 copy-start.4
  205.7 0.4 convert_reduce_fusion
  206.1 0.6 copy-done.1
  206.6 0.0 copy-done.8
  206.6 0.0 copy-start.9
  206.7 0.7 fusion.34
  207.4 0.0 copy-done.4
  207.4 0.9 fusion.33
  208.3 3.3 collective-permute-start
  211.6 0.0 copy-done.9
  211.6 0.9 fusion.2
  212.5 0.1 convert_element_type.145
  212.6 15.2 %all_to_all.31 = bf16[64,1,8]{2,1,0:T(2,128)(2,1)S(1)} all-to-all(bf16[64,1,8]{2,1,0:T(2,128)(2,1)S(1)} %convert_element_type.145), channel_id=1, replica_groups=mesh['section'=8,'expert'=64] {'expert'}, dimensions={0} | all-to-all | bytes 2048 | tf_op jit(solution)/shard_map/all_to_all | solution.py:122
  227.8 0.1 reshape.159
  227.9 0.2 fusion.41
  228.1 0.1 broadcast_in_dim_reshape.3
  228.2 0.7 copy.40
  228.9 127.2 %psum.7 = f32[1,2048]{1,0:T(1,128)} all-reduce(f32[1,2048]{1,0:T(1,128)S(1)} %bitcast.102), channel_id=1, replica_groups=mesh['section'=8,'expert'=64] {'expert'}, use_global_device_ids=true, to_apply=%region_10.11 | all-reduce | flops 2048 | bytes 16384 | tf_op jit(solution)/shard_map/psum | solution.py:143
  356.1 0.0 collective-permute-done
  356.1 0.7 copy.44
  (12 shorter events, 0.2 us)
Async XLA Ops:
  0.6 93.0 %copy-start = (bf16[1,192,2048]{2,1,0:T(8,128)(2,1)S(1)}, bf16[1,192,2048]{2,1,0:T(8,128)(2,1)}, u32[]{:S(2)}) copy-start(bf16[1,192,2048]{2,1,0:T(8,128)(2,1)} %param.13) | copy-start | bytes 2359300
  5.0 23.2 %all-to-all-start = ((bf16[64,1,8]{2,1,0:T(2,128)(2,1)}), bf16[64,1,8]{2,1,0:T(2,128)(2,1)S(1)}, u32[]{:S(2)}, u32[]{:S(2)}) async-start(bf16[64,1,8]{2,1,0:T(2,128)(2,1)} %copy.38), calls=%async_computation | async-start | bytes 65536 | tf_op jit(solution)/shard_map/all_to_all | solution.py:106
  29.9 55.9 %all-to-all-start.2 = ((bf16[64,8,2048]{2,1,0:T(8,128)(2,1)}), bf16[64,8,2048]{2,1,0:T(8,128)(2,1)S(1)}, u32[]{:S(2)}, u32[]{:S(2)}) async-start(bf16[64,8,2048]{2,1,0:T(8,128)(2,1)} %bitcast.14), calls=%async_computation.2 | async-start | bytes 4194304 | tf_op jit(solution)/shard_map/all_to_all | solution.py:104
  85.7 2.0 copy-start.2
  87.7 57.1 %all-to-all-start.1 = ((bf16[64,8,2048]{2,1,0:T(8,128)(2,1)}), bf16[64,8,2048]{2,1,0:T(8,128)(2,1)S(1)}, u32[]{:S(2)}, u32[]{:S(2)}) async-start(bf16[64,8,2048]{2,1,0:T(8,128)(2,1)} %bitcast.8), calls=%async_computation.1 | async-start | bytes 4194304 | tf_op jit(solution)/shard_map/all_to_all | solution.py:105
  93.7 2.6 copy-start.3
  93.7 2.6 copy-start.5
  144.8 2.1 copy-start.7
  146.9 1.1 copy-start.6
  205.7 1.0 copy-start.1
  205.7 1.0 copy-start.8
  205.7 1.7 copy-start.4
  206.6 4.9 %copy-start.9 = (bf16[1,192,2048]{2,1,0:T(8,128)(2,1)S(1)}, bf16[1,192,2048]{2,1,0:T(8,128)(2,1)}, u32[]{:S(2)}) copy-start(bf16[1,192,2048]{2,1,0:T(8,128)(2,1)} %param.15) | copy-start | bytes 2359300
  208.3 147.8 %collective-permute-start = (bf16[64,2048]{1,0:T(8,128)(2,1)}, bf16[64,2048]{1,0:T(8,128)(2,1)S(1)}, u32[]{:S(2)}, u32[]{:S(2)}) collective-permute-start(bf16[64,2048]{1,0:T(8,128)(2,1)} %fusion.33), channel_id=1, source_target_pairs={{64,0},{128,64},{192,128},{256,192},{320,256},{384,320},{448,384},... | collective-permute-start | bytes 786440 | tf_op jit(solution)/shard_map/ppermute | solution.py:14
where the time goes:
time: 357 us
  blocking collectives  199 us (56%)
  waiting for transfers between devices  104 us (29%)
  starting transfers between devices  27.6 us (8%)
  matrix products  12.4 us (3%)
  local copies, waits for them, and re-layouts  9.12 us (3%)
  other arithmetic  3.98 us (1%)
    psum x1, blocking collectives, per_device(): gain_total = lax.psum(gain_correction, 'expert')  127 us
    all_to_all x1, blocking collectives, per_device(): lax.all_to_all(rows_grad.reshape(peers, CAP, width), 'expert', split_axis...  56.9 us
    all_to_all x1, waiting for transfers between devices, per_device(): lax.all_to_all(send_x, 'expert', split_axis=0, concat_axis=0, tiled=True)  49.9 us
    all_to_all x1, waiting for transfers between devices, per_device(): lax.all_to_all(send_dy, 'expert', split_axis=0, concat_axis=0, tiled=True)  46.9 us
    all_to_all x1, blocking collectives, per_device(): lax.all_to_all(comb_part.reshape(peers, CAP), 'expert', split_axis=0, con...  15.2 us
    all_to_all x1, starting transfers between devices, per_device(): lax.all_to_all(send_w, 'expert', split_axis=0, concat_axis=0, tiled=True)  13.8 us
  transfers between devices with their start and end apart: 4, of which 3 were waited for; matrix products, arithmetic and copies ran while one was open for 3% of the time, Pallas kernels for 0%

commit v1 on v0

--- a/solution.py
+++ b/solution.py
@@ -2,6 +2,7 @@
 import jax.numpy as jnp
 from jax import lax
 from jax.sharding import PartitionSpec as P
+from jax.lax import all_gather
 
 EXPERTS = 16
 CAP = 8
@@ -140,7 +141,8 @@
         + reciprocal_norm * (scaled_gradient - normalized_rows * inner_product)
     ).astype(jnp.bfloat16)
     passed = from_behind(input_gradient, "section", -1)
-    gain_total = lax.psum(gain_correction, "expert")
+    push_grid_now = lambda x_in: all_gather(x_in, "expert").sum(axis=0)
+    gain_total = push_grid_now(gain_correction)
     return (passed[None], comb_out[None], gain_total[None])
 
 

time: 357 us -> 276 us (0.77)
  blocking collectives: 199 us -> 47.6 us
  waiting for transfers between devices: 104 us -> 158 us
  starting transfers between devices: 27.6 us -> 40 us
    psum x1 -> x0, blocking collectives: 127 us -> none  [per_device(): gain_total = lax.psum(gain_correction, 'expert')]
    all_to_all x2 -> x0, blocking collectives: 72 us -> none  [the longest x1 56.9 us: per_device(): lax.all_to_all(rows_grad.reshape(peers, CAP, width), 'expert', split_axis...]
    all_to_all x0 -> x2, waiting for transfers between devices: none -> 54.8 us  [the longest x1 50.8 us: per_device(): lax.all_to_all(rows_grad.reshape(peers, CAP, width), 'expert', split_axis...]
    all_gather x0 -> x1, blocking collectives: none -> 47.6 us  [per_device(): push_grid_now = lambda x_in: all_gather(x_in, 'expert').sum(axis=0)]
    all_to_all x0 -> x2, starting transfers between devices: none -> 12.4 us  [the longest x1 6.48 us: per_device(): lax.all_to_all(rows_grad.reshape(peers, CAP, width), 'expert', split_axis...]
  transfers between devices with their start and end apart: 4 -> 6, of which waited for: 3 -> 5; matrix products, arithmetic and copies ran while one was open for 3% -> 5% of each run, Pallas kernels for 0% -> 0%
where the time goes in v1:
time: 276 us; the launch traced here: 275 us
  waiting for transfers between devices  158 us (57%)
  blocking collectives  47.6 us (17%)
  starting transfers between devices  40 us (14%)
  matrix products  15 us (5%)
  local copies, waits for them, and re-layouts  9.26 us (3%)
  other arithmetic  3.91 us (1%)
    all_to_all x1, waiting for transfers between devices, per_device(): lax.all_to_all(rows_grad.reshape(peers, CAP, width), 'expert', split_axis...  50.8 us
    all_to_all x1, waiting for transfers between devices, per_device(): lax.all_to_all(send_x, 'expert', split_axis=0, concat_axis=0, tiled=True)  49.9 us
    all_gather x1, blocking collectives, per_device(): push_grid_now = lambda x_in: all_gather(x_in, 'expert').sum(axis=0)  47.6 us
    all_to_all x1, waiting for transfers between devices, per_device(): lax.all_to_all(send_dy, 'expert', split_axis=0, concat_axis=0, tiled=True)  46.9 us
    all_to_all x1, starting transfers between devices, per_device(): lax.all_to_all(send_w, 'expert', split_axis=0, concat_axis=0, tiled=True)  13.8 us
    all_to_all x1, waiting for transfers between devices, per_device(): lax.all_to_all(send_w, 'expert', split_axis=0, concat_axis=0, tiled=True)  6.72 us
    all_to_all x1, starting transfers between devices, per_device(): lax.all_to_all(rows_grad.reshape(peers, CAP, width), 'expert', split_axis...  6.48 us
    dot_general x3, matrix products, contract_cols(): lax.dot_general(left, right, (((1,), (1,)), ((), ())), preferred_element_...  6.3 us
  transfers between devices with their start and end apart: 6, of which 5 were waited for; matrix products, arithmetic and copies ran while one was open for 5% of the time, Pallas kernels for 0%

profile of v1, /device:TPU:56, one launch (start us, length us, event | category | flops | bytes accessed | tf_op | source)
XLA Modules:
  0.0 275.1 jit_solution(2855866110172505435)
XLA Ops:
  0.6 0.0 copy-start
  0.6 0.8 copy.33
  1.5 0.1 eq.45
  1.6 0.1 eq.49
  1.7 0.8 copy.37
  2.4 0.1 reshape.158
  2.6 1.2 reduce-window.6
  3.7 0.2 slice_reduce_fusion
  4.0 0.1 fusion.52
  4.1 0.2 fusion.14
  4.2 0.1 reshape.143
  4.4 0.6 copy.38
  5.0 13.8 %all-to-all-start = ((bf16[64,1,8]{2,1,0:T(2,128)(2,1)}), bf16[64,1,8]{2,1,0:T(2,128)(2,1)S(1)}, u32[]{:S(2)}, u32[]{:S(2)}) async-start(bf16[64,1,8]{2,1,0:T(2,128)(2,1)} %copy.38), calls=%async_computation | async-start | bytes 65536 | tf_op jit(solution)/shard_map/all_to_all | solution.py:107
  18.8 0.1 reduce_sum.88
  18.9 1.1 fusion.35
  20.0 0.2 fusion.45
  20.2 1.3 fusion.5
  21.5 6.7 %all-to-all-done = bf16[64,1,8]{2,1,0:T(2,128)(2,1)S(1)} async-done(((bf16[64,1,8]{2,1,0:T(2,128)(2,1)}), bf16[64,1,8]{2,1,0:T(2,128)(2,1)S(1)}, u32[]{:S(2)}, u32[]{:S(2)}) %all-to-all-start) | async-done | bytes 1056 | tf_op jit(solution)/shard_map/all_to_all | solution.py:107
  28.2 1.6 broadcast_in_dim.23
  29.9 4.7 %all-to-all-start.2 = ((bf16[64,8,2048]{2,1,0:T(8,128)(2,1)}), bf16[64,8,2048]{2,1,0:T(8,128)(2,1)S(1)}, u32[]{:S(2)}, u32[]{:S(2)}) async-start(bf16[64,8,2048]{2,1,0:T(8,128)(2,1)} %bitcast.14), calls=%async_computation.2 | async-start | bytes 4194304 | tf_op jit(solution)/shard_map/all_to_all | solution.py:105
  34.6 1.3 fusion.4
  35.8 49.9 %all-to-all-done.2 = bf16[64,8,2048]{2,1,0:T(8,128)(2,1)S(1)} async-done(((bf16[64,8,2048]{2,1,0:T(8,128)(2,1)}), bf16[64,8,2048]{2,1,0:T(8,128)(2,1)S(1)}, u32[]{:S(2)}, u32[]{:S(2)}) %all-to-all-start.2) | async-done | bytes 2097184 | tf_op jit(solution)/shard_map/all_to_all | solution.py:105
  85.7 1.8 broadcast_in_dim.22
  87.6 0.2 copy-done.2
  87.7 5.9 %all-to-all-start.1 = ((bf16[64,8,2048]{2,1,0:T(8,128)(2,1)}), bf16[64,8,2048]{2,1,0:T(8,128)(2,1)S(1)}, u32[]{:S(2)}, u32[]{:S(2)}) async-start(bf16[64,8,2048]{2,1,0:T(8,128)(2,1)} %bitcast.8), calls=%async_computation.1 | async-start | bytes 4194304 | tf_op jit(solution)/shard_map/all_to_all | solution.py:106
  93.7 0.0 copy-done
  93.7 0.0 copy-start.3
  93.7 0.0 copy-start.5
  93.7 2.6 fusion.9
  96.3 0.0 copy-done.3
  96.3 0.0 copy-done.5
  96.3 1.6 fusion.11
  97.9 46.9 %all-to-all-done.1 = bf16[64,8,2048]{2,1,0:T(8,128)(2,1)S(1)} async-done(((bf16[64,8,2048]{2,1,0:T(8,128)(2,1)}), bf16[64,8,2048]{2,1,0:T(8,128)(2,1)S(1)}, u32[]{:S(2)}, u32[]{:S(2)}) %all-to-all-start.1) | async-done | bytes 2097184 | tf_op jit(solution)/shard_map/all_to_all | solution.py:106
  144.8 2.1 fusion.2
  146.9 0.7 convert_element_type.145
  147.6 5.9 %all-to-all-start.4 = ((bf16[64,1,8]{2,1,0:T(2,128)(2,1)}), bf16[64,1,8]{2,1,0:T(2,128)(2,1)S(1)}, u32[]{:S(2)}, u32[]{:S(2)}) async-start(bf16[64,1,8]{2,1,0:T(2,128)(2,1)} %convert_element_type.145), calls=%async_computation.4 | async-start | bytes 65536 | tf_op jit(solution)/shard_map/all_to_all | solution.py:123
  153.5 0.0 copy-start.7
  153.5 2.1 fusion.7
  155.6 0.0 copy-done.7
  155.7 0.0 copy-start.6
  155.7 0.8 fusion.17
  156.5 0.3 copy-done.6
  156.8 2.1 fusion.3
  158.9 4.0 %all-to-all-done.4 = bf16[64,1,8]{2,1,0:T(2,128)(2,1)S(1)} async-done(((bf16[64,1,8]{2,1,0:T(2,128)(2,1)}), bf16[64,1,8]{2,1,0:T(2,128)(2,1)S(1)}, u32[]{:S(2)}, u32[]{:S(2)}) %all-to-all-start.4) | async-done | bytes 1056 | tf_op jit(solution)/shard_map/all_to_all | solution.py:123
  163.0 6.5 %all-to-all-start.3 = ((bf16[64,8,2048]{2,1,0:T(8,128)(2,1)}), bf16[64,8,2048]{2,1,0:T(8,128)(2,1)S(1)}, u32[]{:S(2)}, u32[]{:S(2)}) async-start(bf16[64,8,2048]{2,1,0:T(8,128)(2,1)} %fusion.3), calls=%async_computation.3 | async-start | bytes 4194304 | tf_op jit(solution)/shard_map/all_to_all | solution.py:120
  169.4 0.0 copy-start.1
  169.4 0.0 copy-start.8
  169.5 0.1 reshape.160
  169.6 0.0 copy-start.4
  169.6 50.8 %all-to-all-done.3 = bf16[64,8,2048]{2,1,0:T(8,128)(2,1)S(1)} async-done(((bf16[64,8,2048]{2,1,0:T(8,128)(2,1)}), bf16[64,8,2048]{2,1,0:T(8,128)(2,1)S(1)}, u32[]{:S(2)}, u32[]{:S(2)}) %all-to-all-start.3) | async-done | bytes 2097184 | tf_op jit(solution)/shard_map/all_to_all | solution.py:120
  220.4 0.4 convert_reduce_fusion
  220.8 0.0 copy-done.1
  220.8 0.7 fusion.34
  221.6 0.0 copy-done.4
  221.6 0.2 fusion.33
  221.8 3.3 %collective-permute-start = (bf16[64,2048]{1,0:T(8,128)(2,1)S(1)}, bf16[64,2048]{1,0:T(8,128)(2,1)S(1)}, u32[]{:S(2)}, u32[]{:S(2)}) collective-permute-start(bf16[64,2048]{1,0:T(8,128)(2,1)S(1)} %fusion.33), channel_id=1, source_target_pairs={{64,0},{128,64},{192,128},{256,192},{320,256},{384,320},{448,384},... | collective-permute-start | bytes 786440 | tf_op jit(solution)/shard_map/ppermute | solution.py:15
  225.1 0.2 fusion.41
  225.3 0.1 broadcast_in_dim_reshape.3
  225.4 0.7 copy.40
  226.0 47.6 %all-gather = f32[131072]{0:T(1024)S(1)} all-gather(f32[2048]{0:T(1024)S(1)} %get-tuple-element.15), channel_id=2, replica_groups=mesh['section'=8,'expert'=64] {'expert'}, dimensions={0}, use_global_device_ids=true | all-gather | bytes 532480 | tf_op jit(solution)/shard_map/all_gather | solution.py:144
  273.7 0.1 reshape.157
  273.8 0.6 reduce_sum.95
  274.4 0.0 collective-permute-done
  274.4 0.7 copy.44
  (14 shorter events, 0.2 us)
Async XLA Ops:
  0.6 93.0 %copy-start = (bf16[1,192,2048]{2,1,0:T(8,128)(2,1)S(1)}, bf16[1,192,2048]{2,1,0:T(8,128)(2,1)}, u32[]{:S(2)}) copy-start(bf16[1,192,2048]{2,1,0:T(8,128)(2,1)} %param.13) | copy-start | bytes 2359300
  5.0 23.2 %all-to-all-start = ((bf16[64,1,8]{2,1,0:T(2,128)(2,1)}), bf16[64,1,8]{2,1,0:T(2,128)(2,1)S(1)}, u32[]{:S(2)}, u32[]{:S(2)}) async-start(bf16[64,1,8]{2,1,0:T(2,128)(2,1)} %copy.38), calls=%async_computation | async-start | bytes 65536 | tf_op jit(solution)/shard_map/all_to_all | solution.py:107
  29.9 55.9 %all-to-all-start.2 = ((bf16[64,8,2048]{2,1,0:T(8,128)(2,1)}), bf16[64,8,2048]{2,1,0:T(8,128)(2,1)S(1)}, u32[]{:S(2)}, u32[]{:S(2)}) async-start(bf16[64,8,2048]{2,1,0:T(8,128)(2,1)} %bitcast.14), calls=%async_computation.2 | async-start | bytes 4194304 | tf_op jit(solution)/shard_map/all_to_all | solution.py:105
  85.7 2.0 copy-start.2
  87.7 57.1 %all-to-all-start.1 = ((bf16[64,8,2048]{2,1,0:T(8,128)(2,1)}), bf16[64,8,2048]{2,1,0:T(8,128)(2,1)S(1)}, u32[]{:S(2)}, u32[]{:S(2)}) async-start(bf16[64,8,2048]{2,1,0:T(8,128)(2,1)} %bitcast.8), calls=%async_computation.1 | async-start | bytes 4194304 | tf_op jit(solution)/shard_map/all_to_all | solution.py:106
  93.7 2.6 copy-start.3
  93.7 2.6 copy-start.5
  147.6 15.3 %all-to-all-start.4 = ((bf16[64,1,8]{2,1,0:T(2,128)(2,1)}), bf16[64,1,8]{2,1,0:T(2,128)(2,1)S(1)}, u32[]{:S(2)}, u32[]{:S(2)}) async-start(bf16[64,1,8]{2,1,0:T(2,128)(2,1)} %convert_element_type.145), calls=%async_computation.4 | async-start | bytes 65536 | tf_op jit(solution)/shard_map/all_to_all | solution.py:123
  153.5 2.1 copy-start.7
  155.7 1.1 copy-start.6
  163.0 57.5 %all-to-all-start.3 = ((bf16[64,8,2048]{2,1,0:T(8,128)(2,1)}), bf16[64,8,2048]{2,1,0:T(8,128)(2,1)S(1)}, u32[]{:S(2)}, u32[]{:S(2)}) async-start(bf16[64,8,2048]{2,1,0:T(8,128)(2,1)} %fusion.3), calls=%async_computation.3 | async-start | bytes 4194304 | tf_op jit(solution)/shard_map/all_to_all | solution.py:120
  169.4 51.4 %copy-start.1 = (bf16[1,64,2048]{2,1,0:T(8,128)(2,1)S(1)}, bf16[1,64,2048]{2,1,0:T(8,128)(2,1)}, u32[]{:S(2)}) copy-start(bf16[1,64,2048]{2,1,0:T(8,128)(2,1)} %param.8) | copy-start | bytes 786436
  169.4 51.4 %copy-start.8 = (f32[1,2048]{1,0:T(1,128)S(1)}, f32[1,2048]{1,0:T(1,128)}, u32[]{:S(2)}) copy-start(f32[1,2048]{1,0:T(1,128)} %param.10) | copy-start | bytes 24580
  169.6 51.9 %copy-start.4 = (bf16[1,64,2048]{2,1,0:T(8,128)(2,1)S(1)}, bf16[1,64,2048]{2,1,0:T(8,128)(2,1)}, u32[]{:S(2)}) copy-start(bf16[1,64,2048]{2,1,0:T(8,128)(2,1)} %param.9) | copy-start | bytes 786436
  221.8 52.6 %collective-permute-start = (bf16[64,2048]{1,0:T(8,128)(2,1)S(1)}, bf16[64,2048]{1,0:T(8,128)(2,1)S(1)}, u32[]{:S(2)}, u32[]{:S(2)}) collective-permute-start(bf16[64,2048]{1,0:T(8,128)(2,1)S(1)} %fusion.33), channel_id=1, source_target_pairs={{64,0},{128,64},{192,128},{256,192},{320,256},{384,320},{448,384},... | collective-permute-start | bytes 786440 | tf_op jit(solution)/shard_map/ppermute | solution.py:15
